TPU v7x, 32 devices: a whole 2x2x4 slice. The times are simulated.
32 devices in a mesh: tm: 8 (over y, x, core), user: 4 (over z).
Axes of the slice: x: 2, y: 2, z: 4, core: 2. Of those that a mesh axis runs over, the one named last changes fastest.
Arguments:
- events: bfloat16 [4, 8192, 512], P('user', 'tm'), may hold values from -6 to 6
- w_first: bfloat16 [512, 1024], replicated, may hold values from -0.25 to 0.25
- b_first: float32 [1024], replicated, may hold values from -3 to 3
- w_second: bfloat16 [1024, 512], replicated, may hold values from -0.1875 to 0.1875
- count_embed: float32 [512], replicated, may hold values from -0.3 to 0.3
- norm_gain: float32 [512], replicated, may hold values from 0.5 to 1.5
- event_session: int32 [4, 8192], P('user', 'tm'), may hold values from 0 to 511, as said below
- event_count: int32 [4, 8], P('user', 'tm'), may hold values from 256 to 1024, as said below
- session_user: int32 [4, 512], P('user', 'tm'), may hold values from 0 to 65535, as said below
Outputs:
- section_rows: bfloat16 [8, 4, 128, 512], P('tm', 'user')
- section_users: int32 [8, 4, 128], P('tm', 'user')
Inputs may be any that keep to these rules, and one draw needn't show every extreme that they name: `event_session`: the events of time slice t (slots t * 1024 to (t + 1) * 1024 - 1 of a shard) name sessions of slices max(0, t - 4) to t only; some sessions have no valid event. `event_count`: some time slice of some shard has all 1024 events valid. `session_user`: among the 64 sessions of one shard and time slice, at most 32 have users of the same section (user mod 4); in every time slice some section gets exactly 32 from every shard.
All inputs are finite; a program needn't handle non-finite values.
Results may differ from a plain program's by a relative error of at most 0.0042.
Values may be sent and summed in bfloat16 or wider, within the bound.
A program may use at most 64 MiB of HBM per device.

v0:
```python
import jax
import jax.numpy as jnp
from jax import lax
from jax.sharding import PartitionSpec as P


def on_device(
    events,
    w_first,
    b_first,
    w_second,
    count_embed,
    norm_gain,
    event_session,
    event_count,
    session_user,
):
    event_rows = events[0]
    ev_rows = event_rows.shape[0]
    width = event_rows.shape[1]
    sess_dev = session_user.shape[1]
    n_tm = lax.axis_size("tm")
    n_sec = lax.axis_size("user")
    capacity = max(2, 2 * sess_dev // n_sec)
    valid_count = event_count[0, 0]
    hidden = jax.nn.gelu(
        jnp.dot(event_rows, w_first, preferred_element_type=jnp.float32) + b_first
    ).astype(jnp.bfloat16)
    vectors = jnp.dot(hidden, w_second, preferred_element_type=jnp.float32).astype(jnp.bfloat16)
    valid = jnp.arange(ev_rows, dtype=jnp.int32) < valid_count
    session_ids = event_session[0]
    local_ids = jnp.arange(sess_dev, dtype=jnp.int32)
    assign = (
        session_ids[None, :] == jnp.arange(n_tm * sess_dev, dtype=jnp.int32)[:, None]
    ) & valid[None, :]
    partial_value = jnp.dot(
        assign.astype(jnp.bfloat16), vectors, preferred_element_type=jnp.float32
    )
    totals = jnp.sum(assign.astype(jnp.float32), axis=1)
    partial_value, counted = (partial_value, totals)
    sums, totals = (
        lax.psum_scatter(partial_value, "tm", scatter_dimension=0, tiled=True),
        lax.psum_scatter(counted, "tm", scatter_dimension=0, tiled=True),
    )
    averaged = sums / jnp.maximum(totals, 1.0)[:, None]
    mixed = averaged + jnp.log1p(totals)[:, None] * count_embed
    scaled = mixed * lax.rsqrt(jnp.mean(mixed * mixed, axis=-1, keepdims=True) + 1e-06) * norm_gain
    session_rows = scaled.astype(jnp.bfloat16)
    users = session_user[0]
    section = users % n_sec
    same = section[:, None] == section[None, :]
    before = local_ids[:, None] > local_ids[None, :]
    rank = jnp.sum((same & before).astype(jnp.int32), axis=1)
    slot = section * capacity + rank
    assign_slot = slot[None, :] == jnp.arange(n_sec * capacity, dtype=jnp.int32)[:, None]
    outgoing = jnp.dot(
        assign_slot.astype(jnp.bfloat16), session_rows, preferred_element_type=jnp.float32
    )
    outgoing = outgoing.astype(jnp.bfloat16).reshape(n_sec, capacity, width)
    outgoing_users = jnp.sum(jnp.where(assign_slot, users[None, :] + 1, 0), axis=1) - 1
    outgoing_users = outgoing_users.reshape(n_sec, capacity)
    arrived, arrived_users = (
        lax.all_to_all(outgoing, "user", split_axis=0, concat_axis=0, tiled=True),
        lax.all_to_all(outgoing_users, "user", split_axis=0, concat_axis=0, tiled=True),
    )
    section_rows = arrived.reshape(1, 1, n_sec * capacity, width)
    section_users = arrived_users.reshape(1, 1, n_sec * capacity)
    return (section_rows, section_users)


def solution(mesh):
    in_specs = (
        P("user", "tm", None),
        P(),
        P(),
        P(),
        P(),
        P(),
        P("user", "tm"),
        P("user", "tm"),
        P("user", "tm"),
    )
    out_specs = (P("tm", "user", None, None), P("tm", "user", None))
    return jax.shard_map(
        on_device, mesh=mesh, in_specs=in_specs, out_specs=out_specs, check_vma=False
    )
```

profile of v0, /device:TPU:0, one launch (start us, length us, event | category | flops | bytes accessed | tf_op | source)
XLA Modules:
  0.0 74.3 jit_solution(9279864268798132742)
XLA Ops:
  7.2 0.0 copy-start
  7.2 0.0 reduce-scatter.2.cloned.1.call-start
  8.0 0.4 copy-done
  8.4 0.0 copy-start.2
  8.4 4.1 %convolution_convert_fusion = bf16[1024,512]{1,0:T(8,128)(2,1)S(1)} fusion(bf16[1024,512]{1,0:T(8,128)(2,1)S(1)} %copy-done, bf16[512,1024]{1,0:T(8,128)(2,1)} %param.10, f32[1024]{0:T(1024)} %param.11, bf16[1,1024,512]{2,1,0:T(8,128)(2,1)} %param.9), kind=kOutput, calls=%fused_computation.13 | convolution fusion | flops 2158493696 | bytes 4198400 | tf_op jit(solution)/shard_map/dot_general | solution.py:29
  12.5 0.0 copy-done.2
  12.5 1.7 %fusion.9 = f32[512,512]{1,0:T(8,128)} fusion(bf16[1024,512]{1,0:T(8,128)(2,1)S(1)} %convolution_convert_fusion, s32[1024]{0:T(1024)S(1)} %bitcast.27, pred[1024]{0:T(1024)(128)(4,1)S(1)} %iota_compare_fusion.4), kind=kOutput, calls=%fused_computation.12 | convolution fusion | flops 537919488 | bytes 2102272 | tf_op jit(solution)/shard_map/dot_general | solution.py:36
  14.2 0.0 copy-start.4
  14.2 0.0 copy-start.5
  14.2 0.0 copy-start.1
  14.2 0.0 copy-start.3
  14.2 0.0 reduce-scatter.2.cloned.1.call-update
  14.2 0.6 copy-done.4
  14.9 0.2 convert_reduce_fusion.1
  15.1 0.1 select_reduce_fusion
  15.2 0.7 sub.7
  15.8 6.3 %all-to-all-start.1 = ((s32[4,1,32]{2,1,0:T(1,128)}), s32[4,1,32]{2,1,0:T(1,128)S(1)}, u32[]{:S(2)}, u32[]{:S(2)}) async-start(s32[4,1,32]{2,1,0:T(1,128)} %bitcast.10), calls=%async_computation.2 | async-start | bytes 4096 | tf_op jit(solution)/shard_map/all_to_all | solution.py:64
  22.2 0.0 copy-done.5
  22.2 0.6 dynamic-slice
  23.4 0.4 convert_reduce_fusion
  23.8 13.4 %all-reduce = f32[512]{0:T(512)S(1)} all-reduce(f32[512]{0:T(512)S(1)} %convert_reduce_fusion), channel_id=3, replica_groups=mesh['tm'=8,'user'=4] {'tm'}, use_global_device_ids=true, to_apply=%region_3.0.clone | all-reduce | flops 512 | bytes 4096
  37.2 0.1 broadcast_maximum_fusion
  37.3 15.9 %reduce-scatter.2.cloned.1.call-done = f32[64,512]{1,0:T(8,128)} async-done(((f32[512,512]{1,0:T(8,128)}), f32[64,512]{1,0:T(8,128)}) %reduce-scatter.2.cloned.1.call-update) | async-done | bytes 131088 | tf_op jit(solution)/shard_map/reduce_scatter | solution.py:42
  53.2 0.0 copy-done.1
  53.2 1.1 %multiply_reduce_fusion = f32[64]{0:T(128)S(1)} fusion(f32[512]{0:T(512)S(1)} %copy-done.1, f32[64]{0:T(128)S(1)} %get-tuple-element.3, f32[64,512]{1,0:T(8,128)} %reduce-scatter.2.cloned.1.call-done, f32[64]{0:T(128)S(1)} %get-tuple-element.2), kind=kLoop, calls=%fused_computation.19 | loop fusion | flops 163776 | bytes 133888 | tf_op jit(solution)/shard_map/reduce_sum | solution.py:47
  54.3 0.0 copy-done.3
  54.3 1.9 %convolution_convert_fusion.1 = bf16[128,512]{1,0:T(8,128)(2,1)} fusion(f32[512]{0:T(512)S(1)} %copy-done.3, f32[64]{0:T(128)S(1)} %add_rsqrt_fusion, s32[64]{0:T(128)S(1)} %fusion.22, f32[64,512]{1,0:T(8,128)} %reduce-scatter.2.cloned.1.call-done, f32[512]{0:T(512)S(1)} %copy-done.1, f32[64]{0:T(128)S(1)} %get-tuple-element.3, f32[64]{0:T(128)S(1)} %get-tuple-element.2), kind=kOutput, calls=%fused_computation.14 | convolution fusion | flops 8658944 | bytes 267264 | tf_op jit(solution)/shard_map/dot_general | solution.py:56
  56.1 0.0 all-to-all-done.1
  56.2 4.6 %all-to-all-start = ((bf16[4,32,512]{2,1,0:T(8,128)(2,1)}), bf16[4,32,512]{2,1,0:T(8,128)(2,1)S(1)}, u32[]{:S(2)}, u32[]{:S(2)}) async-start(bf16[4,32,512]{2,1,0:T(8,128)(2,1)} %bitcast.7), calls=%async_computation.1 | async-start | bytes 262144 | tf_op jit(solution)/shard_map/all_to_all | solution.py:63
  60.8 0.5 broadcast.80
  61.3 0.7 reduce.3
  61.9 0.6 reshape.71
  62.5 4.3 %all-to-all-done = bf16[4,32,512]{2,1,0:T(8,128)(2,1)S(1)} async-done(((bf16[4,32,512]{2,1,0:T(8,128)(2,1)}), bf16[4,32,512]{2,1,0:T(8,128)(2,1)S(1)}, u32[]{:S(2)}, u32[]{:S(2)}) %all-to-all-start) | async-done | bytes 131104 | tf_op jit(solution)/shard_map/all_to_all | solution.py:63
  66.8 0.7 copy.15
  (6 shorter events, 0.0 us)
Async XLA Ops:
  7.2 1.2 %copy-start = (bf16[1024,512]{1,0:T(8,128)(2,1)S(1)}, bf16[1024,512]{1,0:T(8,128)(2,1)}, u32[]{:S(2)}) copy-start(bf16[1024,512]{1,0:T(8,128)(2,1)} %param.12) | copy-start | bytes 3145732
  7.2 46.0 %reduce-scatter.2.cloned.1.call-start = ((), (), s32[]{:S(2)}) async-start(), calls=%async_computation.3 | async-start | bytes 1179648 | tf_op jit(solution)/shard_map/reduce_scatter | solution.py:42
  8.4 4.1 %copy-start.2 = (s32[1,1024]{1,0:T(1,128)S(1)}, s32[1,1024]{1,0:T(1,128)}, u32[]{:S(2)}) copy-start(s32[1,1024]{1,0:T(1,128)} %param.15) | copy-start | bytes 12292
  14.2 0.7 copy-start.4
  14.2 8.0 %copy-start.5 = (u32[32]{0:T(128)S(1)}, u32[32]{0:T(128)}, u32[]{:S(2)}) copy-start(u32[32]{0:T(128)} %constant.47) | copy-start | bytes 388
  14.2 39.0 %copy-start.1 = (f32[512]{0:T(512)S(1)}, f32[512]{0:T(512)}, u32[]{:S(2)}) copy-start(f32[512]{0:T(512)} %param.13) | copy-start | bytes 6148
  14.2 40.1 %copy-start.3 = (f32[512]{0:T(512)S(1)}, f32[512]{0:T(512)}, u32[]{:S(2)}) copy-start(f32[512]{0:T(512)} %param.14) | copy-start | bytes 6148
  15.8 40.3 %all-to-all-start.1 = ((s32[4,1,32]{2,1,0:T(1,128)}), s32[4,1,32]{2,1,0:T(1,128)S(1)}, u32[]{:S(2)}, u32[]{:S(2)}) async-start(s32[4,1,32]{2,1,0:T(1,128)} %bitcast.10), calls=%async_computation.2 | async-start | bytes 4096 | tf_op jit(solution)/shard_map/all_to_all | solution.py:64
  56.2 10.7 %all-to-all-start = ((bf16[4,32,512]{2,1,0:T(8,128)(2,1)}), bf16[4,32,512]{2,1,0:T(8,128)(2,1)S(1)}, u32[]{:S(2)}, u32[]{:S(2)}) async-start(bf16[4,32,512]{2,1,0:T(8,128)(2,1)} %bitcast.7), calls=%async_computation.1 | async-start | bytes 262144 | tf_op jit(solution)/shard_map/all_to_all | solution.py:63
Sparse Core Ops, SparseCore 0:
  14.4 38.7 reduce-scatter.1
where the time goes:
time: 74.8 us; the launch traced here: 74.3 us
  waiting for transfers between devices  20.2 us (27%)
  between operations  15.5 us (21%)
  blocking collectives  13.4 us (18%)
  starting transfers between devices  11 us (15%)
  matrix products  7.63 us (10%)
  local copies, waits for them, and re-layouts  4.1 us (5%)
  other arithmetic  2.59 us (3%)
    reduce_scatter x1, waiting for transfers between devices, on_device(): lax.psum_scatter(partial_value, 'tm', scatter_dimension=0, tiled=True)  15.9 us
    unnamed x1, blocking collectives  13.4 us
    all_to_all x1, starting transfers between devices, on_device(): lax.all_to_all(outgoing_users, 'user', split_axis=0, concat_axis=0, tiled...  6.32 us
    all_to_all x1, starting transfers between devices, on_device(): lax.all_to_all(outgoing, 'user', split_axis=0, concat_axis=0, tiled=True)  4.61 us
    all_to_all x1, waiting for transfers between devices, on_device(): lax.all_to_all(outgoing, 'user', split_axis=0, concat_axis=0, tiled=True)  4.3 us
    dot_general x1, matrix products, on_device(): jnp.dot(hidden, w_second, preferred_element_type=jnp.float32)  4.06 us
    unnamed x14, local copies, waits for them, and re-layouts  2.33 us
    dot_general x1, matrix products, on_device(): jnp.dot(assign_slot.astype(jnp.bfloat16), session_rows, preferred_element...  1.86 us
  transfers between devices with their start and end apart: 3, of which 2 were waited for; matrix products, arithmetic and copies ran while one was open for 9% of the time, Pallas kernels for 0%

commit v1 on v0

v1 whole, which is shorter than its diff:
```python
import functools
import math

import jax
import jax.numpy as jnp
from jax import lax
from jax.experimental import pallas as pl
from jax.experimental.pallas import tpu as pltpu
from jax.sharding import PartitionSpec as P

MESH = pl.DeviceIdType.MESH
BF16 = jnp.bfloat16
F32 = jnp.float32
I32 = jnp.int32


def iota(shape, axis):
    return lax.broadcasted_iota(I32, shape, axis)


def kernel(
    n_tm,
    n_sec,
    reach,
    cap,
    events,
    w_first,
    w_second,
    b_first,
    count_embed,
    norm_gain,
    event_session,
    event_count,
    session_user,
    out_rows,
    out_users,
    ev_v,
    w1_v,
    w2_v,
    acc,
    cnt,
    sums_send,
    sums_recv,
    cnt_recv,
    rows_send,
    rows_recv,
    users_send,
    users_recv,
    load_sem,
    sums_ss,
    sums_rs,
    cnt_ss,
    cnt_rs,
    rows_ss,
    rows_rs,
    users_ss,
    users_rs,
):
    t = lax.axis_index("tm")
    u = lax.axis_index("user")
    ev_rows, width = ev_v.shape
    hidden = w1_v.shape[1]
    sess = session_user.shape[1]
    held = (reach + 1) * sess
    step = min(256, hidden)

    loads = []
    pairs = ((w_first, w1_v), (events.at[0], ev_v), (w_second, w2_v))
    for i, (src, dst) in enumerate(pairs):
        load = pltpu.make_async_copy(src, dst, load_sem.at[i])
        load.start()
        loads.append(load)

    barrier = pltpu.get_barrier_semaphore()
    for d in range(1, reach + 1):

        @pl.when(t + d < n_tm)
        def _(d=d):
            pl.semaphore_signal(
                barrier, inc=1, device_id={"tm": t + d}, device_id_type=MESH
            )

    for k in range(1, n_sec):
        pl.semaphore_signal(
            barrier,
            inc=1,
            device_id={"user": lax.rem(u + k, n_sec)},
            device_id_type=MESH,
        )

    def sums_copy(d):
        return pltpu.make_async_remote_copy(
            src_ref=sums_send.at[d - 1],
            dst_ref=sums_recv.at[d - 1],
            send_sem=sums_ss.at[d - 1],
            recv_sem=sums_rs.at[d - 1],
            device_id={"tm": t - d},
            device_id_type=MESH,
        )

    def cnt_copy(d):
        return pltpu.make_async_remote_copy(
            src_ref=cnt.at[d],
            dst_ref=cnt_recv.at[d - 1],
            send_sem=cnt_ss.at[d - 1],
            recv_sem=cnt_rs.at[d - 1],
            device_id={"tm": t - d},
            device_id_type=MESH,
        )

    def routed_copy(k, send, recv, ss, rs):
        v = lax.rem(u + k, n_sec)
        return pltpu.make_async_remote_copy(
            src_ref=send.at[v],
            dst_ref=recv.at[u],
            send_sem=ss.at[k - 1],
            recv_sem=rs.at[k - 1],
            device_id={"user": v},
            device_id_type=MESH,
        )

    def rows_copy(k):
        return routed_copy(k, rows_send, rows_recv, rows_ss, rows_rs)

    def users_copy(k):
        return routed_copy(k, users_send, users_recv, users_ss, users_rs)

    ids = event_session[...]
    block = t - ids // sess
    local = block * sess + lax.rem(ids, sess)
    lane = iota((1, ev_rows), 1)
    local = jnp.where(lane < event_count[...], local, -1)
    belongs = jnp.where(local == iota((held, ev_rows), 0), 1.0, 0.0)
    assign = belongs.astype(BF16)
    totals = jnp.sum(belongs, axis=1, keepdims=True)
    cnt[...] = jnp.broadcast_to(totals, (held, 128)).reshape(reach + 1, sess, 128)

    user_row = session_user[...]
    square = iota((sess, sess), 0), iota((sess, sess), 1)
    user_col = jnp.sum(
        jnp.where(square[0] == square[1], user_row, 0), axis=1, keepdims=True
    )
    sec_row = lax.rem(user_row, n_sec)
    sec_col = lax.rem(user_col, n_sec)
    same = jnp.where(sec_row == sec_col, 1, 0)
    rank_row = jnp.sum(
        jnp.where(square[0] < square[1], same, 0), axis=0, keepdims=True
    )
    rank_col = jnp.sum(
        jnp.where(square[1] < square[0], same, 0), axis=1, keepdims=True
    )
    padded = rows_send.shape[1]
    place = jnp.where(
        sec_row * padded + rank_row == iota((n_sec * padded, sess), 0), 1.0, 0.0
    ).astype(BF16)
    slots = n_sec * cap
    at = iota((sess, slots), 1) == rank_col + u * cap
    for v in range(n_sec):
        named = jnp.where(at & (sec_col == v), user_col + 1, 0)
        users_send[v] = jnp.broadcast_to(
            jnp.sum(named, axis=0, keepdims=True), (8, slots)
        )

    c_one = math.sqrt(2.0 / math.pi)
    c_three = c_one * 0.044715

    def part(i):
        cols = slice(i * step, (i + 1) * step)
        x = jnp.dot(ev_v[...], w1_v[:, cols], preferred_element_type=F32)
        x = x + b_first[:, cols]
        twice = x + x * jnp.tanh(x * (c_one + c_three * (x * x)))
        pooled = jnp.dot(assign, twice.astype(BF16), preferred_element_type=F32)
        return jnp.dot(pooled.astype(BF16), w2_v[cols, :], preferred_element_type=F32)

    loads[0].wait()
    loads[1].wait()
    loads[2].wait()
    acc[...] = part(0)

    pl.semaphore_wait(barrier, jnp.minimum(t, reach) + n_sec - 1)
    for k in range(1, n_sec):
        users_copy(k).start()
    for d in range(reach, 0, -1):

        @pl.when(t >= d)
        def _(d=d):
            cnt_copy(d).start()

    for i in range(1, hidden // step):
        acc[...] += part(i)

    for d in range(reach, 0, -1):

        @pl.when(t >= d)
        def _(d=d):
            sums_send[d - 1] = acc[d * sess : (d + 1) * sess].astype(BF16)
            sums_copy(d).start()

    for d in range(1, reach + 1):

        @pl.when(t + d < n_tm)
        def _(d=d):
            cnt_copy(d).wait_recv()
            sums_copy(d).wait_recv()
            acc[:sess] += sums_recv[d - 1].astype(F32)
            cnt[0] += cnt_recv[d - 1]

    count = cnt[0][:, :1]
    mixed = acc[:sess] * (0.5 / jnp.maximum(count, 1.0))
    mixed = mixed + jnp.log(1.0 + count) * count_embed[...]
    mean = jnp.mean(mixed * mixed, axis=1, keepdims=True)
    rows = (mixed * lax.rsqrt(mean + 1e-06) * norm_gain[...]).astype(BF16)
    outgoing = jnp.dot(place, rows, preferred_element_type=F32).astype(BF16)
    rows_send[...] = outgoing.reshape(n_sec, padded, width)
    for k in range(1, n_sec):
        rows_copy(k).start()
    rows_recv[u] = rows_send[u]
    users_recv[u] = users_send[u]

    for k in range(1, n_sec):
        users_copy(k).wait_recv()
    out_users[0] = jnp.sum(users_recv[...], axis=0)[:1] - 1
    for k in range(1, n_sec):
        rows_copy(k).wait_recv()
    if padded == cap:
        out_rows[0, 0] = rows_recv[...].reshape(slots, width)
    else:
        kept = rows_recv[...].astype(F32)[:, :cap]
        out_rows[0, 0] = kept.reshape(slots, width).astype(BF16)

    for d in range(1, reach + 1):

        @pl.when(t >= d)
        def _(d=d):
            cnt_copy(d).wait_send()
            sums_copy(d).wait_send()

    for k in range(1, n_sec):
        users_copy(k).wait_send()
        rows_copy(k).wait_send()


def on_device(
    n_tm,
    n_sec,
    events,
    w_first,
    b_first,
    w_second,
    count_embed,
    norm_gain,
    event_session,
    event_count,
    session_user,
):
    _, ev_rows, width = events.shape
    hidden = w_first.shape[1]
    sess = session_user.shape[1]
    reach = n_tm // 2
    cap = max(2, 2 * sess // n_sec)
    padded = -(-cap // 16) * 16
    slots = n_sec * cap
    held = (reach + 1) * sess
    dma = pltpu.SemaphoreType.DMA
    vmem = pl.BlockSpec(memory_space=pltpu.VMEM)
    hbm = pl.BlockSpec(memory_space=pl.ANY)
    return pl.pallas_call(
        functools.partial(kernel, n_tm, n_sec, reach, cap),
        out_shape=(
            jax.ShapeDtypeStruct((1, 1, slots, width), BF16),
            jax.ShapeDtypeStruct((1, 1, slots), I32),
        ),
        in_specs=[hbm] * 3 + [vmem] * 6,
        out_specs=(vmem, vmem),
        scratch_shapes=[
            pltpu.VMEM((ev_rows, width), BF16),
            pltpu.VMEM((width, hidden), BF16),
            pltpu.VMEM((hidden, width), BF16),
            pltpu.VMEM((held, width), F32),
            pltpu.VMEM((reach + 1, sess, 128), F32),
            pltpu.VMEM((reach, sess, width), BF16),
            pltpu.VMEM((reach, sess, width), BF16),
            pltpu.VMEM((reach, sess, 128), F32),
            pltpu.VMEM((n_sec, padded, width), BF16),
            pltpu.VMEM((n_sec, padded, width), BF16),
            pltpu.VMEM((n_sec, 8, slots), I32),
            pltpu.VMEM((n_sec, 8, slots), I32),
            dma((3,)),
            dma((reach,)),
            dma((reach,)),
            dma((reach,)),
            dma((reach,)),
            dma((n_sec - 1,)),
            dma((n_sec - 1,)),
            dma((n_sec - 1,)),
            dma((n_sec - 1,)),
        ],
        compiler_params=pltpu.CompilerParams(
            collective_id=0, has_side_effects=True, vmem_limit_bytes=48 << 20
        ),
        name="pool_and_route",
    )(
        events,
        w_first,
        w_second,
        b_first.reshape(1, hidden),
        count_embed.reshape(1, width),
        norm_gain.reshape(1, width),
        event_session,
        event_count,
        session_user,
    )


def solution(mesh):
    in_specs = (
        P("user", "tm", None),
        P(),
        P(),
        P(),
        P(),
        P(),
        P("user", "tm"),
        P("user", "tm"),
        P("user", "tm"),
    )
    out_specs = (P("tm", "user", None, None), P("tm", "user", None))
    return jax.shard_map(
        functools.partial(on_device, mesh.shape["tm"], mesh.shape["user"]),
        mesh=mesh,
        in_specs=in_specs,
        out_specs=out_specs,
        check_vma=False,
    )
```

time: 74.8 us -> 26.5 us (0.35)
  the two profiles are of different devices: /device:TPU:0 before, /device:TPU:2 now
where the time goes in v1:
time: 26.5 us; the launch traced here: 26.2 us
  Pallas kernels  18 us (68%)
  local copies, waits for them, and re-layouts  6.87 us (26%)
  between operations  1.34 us (5%)
    pallas_call x1, Pallas kernels, on_device(): pl.pallas_call(functools.partial(kernel, n_tm, n_sec, reach, cap), out_sh...  18 us
    unnamed x18, local copies, waits for them, and re-layouts  6.87 us

profile of v1, /device:TPU:2, one launch (start us, length us, event | category | flops | bytes accessed | tf_op | source)
XLA Modules:
  0.0 26.2 jit_solution(5229511334656911261)
XLA Ops:
  0.6 0.0 copy-start.3
  1.3 0.0 copy-start.5
  1.3 0.0 copy-start.7
  1.3 0.0 copy-done.3
  1.3 0.7 %copy-done.5 = f32[512]{0:T(512)S(1)} copy-done((f32[512]{0:T(512)S(1)}, f32[512]{0:T(512)}, u32[]{:S(2)}) %copy-start.5) | copy-done | bytes 2072
  2.0 0.0 copy-done.7
  2.0 0.0 copy-start
  2.0 1.2 %copy-done = bf16[1,1024,512]{2,1,0:T(8,128)(2,1)S(1)} copy-done((bf16[1,1024,512]{2,1,0:T(8,128)(2,1)S(1)}, bf16[1,1024,512]{2,1,0:T(8,128)(2,1)}, u32[]{:S(2)}) %copy-start) | copy-done | bytes 1048600
  3.2 0.0 copy-start.1
  3.2 1.2 %copy-done.1 = bf16[512,1024]{1,0:T(8,128)(2,1)S(1)} copy-done((bf16[512,1024]{1,0:T(8,128)(2,1)S(1)}, bf16[512,1024]{1,0:T(8,128)(2,1)}, u32[]{:S(2)}) %copy-start.1) | copy-done | bytes 1048600
  4.4 0.0 copy-start.2
  4.4 1.2 %copy-done.2 = bf16[1024,512]{1,0:T(8,128)(2,1)S(1)} copy-done((bf16[1024,512]{1,0:T(8,128)(2,1)S(1)}, bf16[1024,512]{1,0:T(8,128)(2,1)}, u32[]{:S(2)}) %copy-start.2) | copy-done | bytes 1048600
  5.7 0.0 copy-start.4
  5.7 0.7 %copy-done.4 = s32[1,1024]{1,0:T(1,128)S(1)} copy-done((s32[1,1024]{1,0:T(1,128)S(1)}, s32[1,1024]{1,0:T(1,128)}, u32[]{:S(2)}) %copy-start.4) | copy-done | bytes 4120
  6.4 0.0 copy-start.6
  6.4 0.7 %copy-done.6 = f32[512]{0:T(512)S(1)} copy-done((f32[512]{0:T(512)S(1)}, f32[512]{0:T(512)}, u32[]{:S(2)}) %copy-start.6) | copy-done | bytes 2072
  7.0 18.0 %pool_and_route.1 = (bf16[1,1,128,512]{3,2,1,0:T(8,128)(2,1)S(1)}, s32[1,1,128]{2,1,0:T(1,128)S(1)}) custom-call(bf16[1,1024,512]{2,1,0:T(8,128)(2,1)S(1)} %copy-done, bf16[512,1024]{1,0:T(8,128)(2,1)S(1)} %copy-done.1, bf16[1024,512]{1,0:T(8,128)(2,1)S(1)} %copy-done.2, f32[1,1024]{1,0:T(1,128)S(1)} %bitcast.3, f32[1,512]{1,0:T(1,128)S(1)} %bitcast.4, ...), custom_call_target="tpu_custom_call" | custom-call | tf_op jit(solution)/shard_map/pool_and_route/pallas_call | solution.py:267
  25.0 0.7 %copy.14 = bf16[1,1,128,512]{3,2,1,0:T(8,128)(2,1)} copy(bf16[1,1,128,512]{3,2,1,0:T(8,128)(2,1)S(1)} %get-tuple-element.4) | data formatting | bytes 262144
  25.7 0.5 %copy.15 = s32[1,1,128]{2,1,0:T(1,128)} copy(s32[1,1,128]{2,1,0:T(1,128)S(1)} %get-tuple-element.5) | data formatting | bytes 1024
Async XLA Ops:
  0.6 0.7 %copy-start.3 = (f32[1024]{0:T(1024)S(1)}, f32[1024]{0:T(1024)}, u32[]{:S(2)}) copy-start(f32[1024]{0:T(1024)} %param.11) | copy-start | bytes 12292
  1.3 0.7 %copy-start.5 = (f32[512]{0:T(512)S(1)}, f32[512]{0:T(512)}, u32[]{:S(2)}) copy-start(f32[512]{0:T(512)} %param.13) | copy-start | bytes 6148
  1.3 0.7 %copy-start.7 = (s32[1,64]{1,0:T(1,128)S(1)}, s32[1,64]{1,0:T(1,128)}, u32[]{:S(2)}) copy-start(s32[1,64]{1,0:T(1,128)} %session_user.1) | copy-start | bytes 772
  2.0 1.2 %copy-start = (bf16[1,1024,512]{2,1,0:T(8,128)(2,1)S(1)}, bf16[1,1024,512]{2,1,0:T(8,128)(2,1)}, u32[]{:S(2)}) copy-start(bf16[1,1024,512]{2,1,0:T(8,128)(2,1)} %events.1) | copy-start | bytes 3145732
  3.2 1.2 %copy-start.1 = (bf16[512,1024]{1,0:T(8,128)(2,1)S(1)}, bf16[512,1024]{1,0:T(8,128)(2,1)}, u32[]{:S(2)}) copy-start(bf16[512,1024]{1,0:T(8,128)(2,1)} %w_first.1) | copy-start | bytes 3145732
  4.4 1.2 %copy-start.2 = (bf16[1024,512]{1,0:T(8,128)(2,1)S(1)}, bf16[1024,512]{1,0:T(8,128)(2,1)}, u32[]{:S(2)}) copy-start(bf16[1024,512]{1,0:T(8,128)(2,1)} %w_second.1) | copy-start | bytes 3145732
  5.7 0.7 %copy-start.4 = (s32[1,1024]{1,0:T(1,128)S(1)}, s32[1,1024]{1,0:T(1,128)}, u32[]{:S(2)}) copy-start(s32[1,1024]{1,0:T(1,128)} %event_session.1) | copy-start | bytes 12292
  6.4 0.7 %copy-start.6 = (f32[512]{0:T(512)S(1)}, f32[512]{0:T(512)}, u32[]{:S(2)}) copy-start(f32[512]{0:T(512)} %param.14) | copy-start | bytes 6148
